TPU v7x, 1024 devices: a whole 4x4x32 slice. The times are simulated.
1024 devices in a mesh: row: 32 (over x, z_hi, core), col: 32 (over y, z_lo).
Axes of the slice: x: 4, y: 4, z: 32 (z_hi: 4, z_lo: 8; z = z_hi * 8 + z_lo), core: 2. Of those that a mesh axis runs over, the one named last changes fastest.
Arguments:
- left_blocks: bfloat16 [32, 32, 24, 128, 128], P('row', 'col'), may hold values from -0.5 to 0.5
- left_where: int32 [32, 32, 24], P('row', 'col'), may hold values from 0 to 48, as said below
- right_blocks: bfloat16 [32, 32, 32, 128, 128], P('row', 'col'), may hold values from -6 to 6
- right_where: int32 [32, 32, 32], P('row', 'col'), may hold values from 0 to 64, as said below
- keep_where: int32 [32, 32, 24], P('row', 'col'), may hold values from 0 to 47, as said below
Outputs:
- result_blocks: float32 [32, 32, 24, 128, 128], P('row', 'col')
Inputs may be any that keep to these rules, and one draw needn't show every extreme that they name: `left_where`: in each grid position the live slots name distinct block positions; empty slots hold 48; at least 12 slots of every panel are live, and some panel has all of them live. `right_where`: in each grid position the live slots name distinct block positions; empty slots hold 64; at least 16 slots of every panel are live, and some panel has all of them live. `keep_where`: distinct within each grid position.
All inputs are finite; a program needn't handle non-finite values.
Results may differ from a plain program's by a relative error of at most 0.0003.
Values may be sent and summed in bfloat16 or wider, within the bound.
No kernel may reach another device: no remote copies, remote signals or barrier semaphores. Data moves between devices by JAX's collectives and lax.ppermute only.
A program may use at most 32 MiB of HBM per device.

v0:
```python
import jax
import jax.numpy as jnp
from jax import lax
from jax.experimental import pallas as pl
from jax.experimental.pallas import tpu as pltpu
from jax.sharding import PartitionSpec as P

BLK = 128
MB = 6
KW = 8
NB = 8
SLOTS_A = 24
SLOTS_B = 32
SLOTS_C = 24
STEP = 2
AXES = ("row", "col")
VMEM_LIMIT = 40 * 1024 * 1024

SMEM_SPEC = pl.BlockSpec(memory_space=pltpu.SMEM)
VMEM_SPEC = pl.BlockSpec(memory_space=pltpu.VMEM)
ANY_SPEC = pl.BlockSpec(memory_space=pl.ANY)


def plan_kernel(across, rw, rw2, kw, lw2, told, blocks, meta, packed, left_mask, keep_mask, sems):
    sends = across[0] == 0

    def right_at(s):
        return jnp.where(sends, rw[s], rw2[s])

    def keep_at(u):
        return jnp.where(sends, told[u], kw[u])

    def left_at(s):
        return jnp.where(sends, told[SLOTS_C + s], lw2[s])

    for k in range(KW + 1):
        left_mask[k] = 0
    for j in range(NB):
        keep_mask[j] = 0
    for s in range(SLOTS_A):
        w = left_at(s)
        bit = jnp.where(w < MB * KW, lax.shift_left(jnp.int32(1), w >> 3), 0)
        left_mask[w & 7] = left_mask[w & 7] | bit
    for u in range(SLOTS_C):
        w = keep_at(u)
        keep_mask[w & 7] = keep_mask[w & 7] | lax.shift_left(jnp.int32(1), w >> 3)

    def copy(s, n):
        return pltpu.make_async_copy(blocks.at[s], packed.at[n], sems.at[n])

    n = jnp.int32(0)
    for s in range(SLOTS_B):
        w = right_at(s)
        need = (left_mask[w >> 3] & keep_mask[w & 7]) != 0

        @pl.when(need)
        def _(s=s, n=n, w=w):
            meta[1 + n] = w

            @pl.when(sends)
            def _():
                copy(s, n).start()

        n = n + need.astype(jnp.int32)
    meta[0] = n

    @pl.when(sends)
    def _():
        @pl.loop(0, n)
        def _(t):
            copy(0, t).wait()


def fill_right(panel, where_at, blocks, count):
    @pl.loop(0, count)
    def _(s):
        w = where_at(s)
        at = pl.multiple_of((w >> 3) * BLK, BLK)
        panel[w & 7, pl.ds(at, BLK), :] = blocks[s]


def fill_left(panel, where, blocks):
    @pl.loop(0, MB + 1)
    def _(i):
        panel[i] = jnp.zeros(panel.shape[1:], panel.dtype)

    @pl.loop(0, SLOTS_A)
    def _(s):
        w = where[s]
        at = pl.multiple_of((w & 7) * BLK, BLK)
        panel[w >> 3, :, pl.ds(at, BLK)] = blocks[s]


def clear_right(panel):
    @pl.loop(0, NB)
    def _(j):
        panel[j] = jnp.zeros(panel.shape[1:], panel.dtype)


def block_product(left, right, w):
    return jnp.dot(
        left[w >> 3], right[w & 7, : KW * BLK, :], preferred_element_type=jnp.float32
    )


def own_kernel(lw, rw, kw, left_blocks, right_blocks, total, left, right):
    fill_left(left, lw, left_blocks)
    clear_right(right)
    fill_right(right, lambda s: rw[s], right_blocks, SLOTS_B)

    @pl.loop(0, SLOTS_C)
    def _(u):
        total[u] = block_product(left, right, kw[u])


def right_kernel(across, meta, rw, arrived, beside, right):
    clear_right(right)

    @pl.when(across[0] == 0)
    def _():
        fill_right(right, lambda s: rw[s], beside, SLOTS_B)

    @pl.when(across[0] != 0)
    def _():
        fill_right(right, lambda s: meta[1 + s], arrived, meta[0])


def last_kernel(lw, kw, left_blocks, right, total, out, left):
    fill_left(left, lw, left_blocks)
    for u in range(SLOTS_C):
        out[u] = total[u] + block_product(left, right, kw[u])


def call(kernel, out_shape, in_specs, out_specs, scratch, flops, moved):
    return pl.pallas_call(
        kernel,
        out_shape=out_shape,
        in_specs=in_specs,
        out_specs=out_specs,
        scratch_shapes=scratch,
        compiler_params=pltpu.CompilerParams(vmem_limit_bytes=VMEM_LIMIT),
        cost_estimate=pl.CostEstimate(flops=flops, bytes_accessed=moved, transcendentals=0),
    )


LEFT_PANEL = (MB + 1, BLK, KW * BLK)
RIGHT_PANEL = (NB, (KW + 1) * BLK, BLK)
FLOPS = 2 * SLOTS_C * KW * BLK**3


def on_device(left_blocks, left_where, right_blocks, right_where, keep_where):
    lb, lw = left_blocks[0, 0], left_where[0, 0]
    rb, rw = right_blocks[0, 0], right_where[0, 0]
    kw = keep_where[0, 0]
    rows, cols = lax.axis_size("row"), lax.axis_size("col")

    def at(p, q):
        return (p % rows) * cols + q % cols

    grid = [(p, q) for p in range(rows) for q in range(cols)]
    across = [(at(p + 1, q), at(p, q)) for p, q in grid if p % 2 == 1]
    beside = [(at(p + 1, q), at(p, q)) for p, q in grid if p % 2 == 0]
    back = [(b, a) for a, b in across]
    left_on = [(at(p, q + 1), at(p, q)) for p, q in grid]
    side = (lax.axis_index("row") % 2).astype(jnp.int32)[None]

    lw2 = lax.ppermute(lw, AXES, left_on)
    rw2 = lax.ppermute(rw, AXES, across + beside)
    told = lax.ppermute(jnp.concatenate([kw, lw2]), AXES, back)
    lb_sent, _ = lax.optimization_barrier((lb, (lw2, rw2)))
    lb2 = lax.ppermute(lb_sent, AXES, left_on)
    beside_blocks = lax.ppermute(rb, AXES, beside)

    meta, packed = call(
        plan_kernel,
        (
            jax.ShapeDtypeStruct((SLOTS_B + 1,), jnp.int32),
            jax.ShapeDtypeStruct(rb.shape, rb.dtype),
        ),
        [SMEM_SPEC] * 6 + [ANY_SPEC],
        (SMEM_SPEC, VMEM_SPEC),
        [
            pltpu.SMEM((KW + 1,), jnp.int32),
            pltpu.SMEM((NB,), jnp.int32),
            pltpu.SemaphoreType.DMA((SLOTS_B,)),
        ],
        0,
        2 * rb.size,
    )(side, rw, rw2, kw, lw2, told, rb)

    def branch(size):
        def body(packed, meta, rw2, beside_blocks, lb, lw, rb, rw, kw):
            arrived = lax.ppermute(packed[:size], AXES, across)
            total = call(
                own_kernel,
                jax.ShapeDtypeStruct((SLOTS_C, BLK, BLK), jnp.float32),
                [SMEM_SPEC] * 3 + [VMEM_SPEC] * 2,
                VMEM_SPEC,
                [pltpu.VMEM(LEFT_PANEL, lb.dtype), pltpu.VMEM(RIGHT_PANEL, rb.dtype)],
                FLOPS,
                4 * SLOTS_C * BLK * BLK,
            )(lw, rw, kw, lb, rb)
            right = call(
                right_kernel,
                jax.ShapeDtypeStruct(RIGHT_PANEL, rb.dtype),
                [SMEM_SPEC] * 3 + [VMEM_SPEC] * 2,
                VMEM_SPEC,
                [],
                0,
                2 * rb.size,
            )(side, meta, rw2, arrived, beside_blocks)
            return total, right

        return body

    sizes = range(STEP, SLOTS_B + 1, STEP)
    pick = jnp.maximum((meta[0] + (STEP - 1)) // STEP, 1) - 1
    total, right = lax.switch(
        pick,
        [branch(size) for size in sizes],
        packed, meta, rw2, beside_blocks, lb, lw, rb, rw, kw,
    )
    out = call(
        last_kernel,
        jax.ShapeDtypeStruct((SLOTS_C, BLK, BLK), jnp.float32),
        [SMEM_SPEC] * 2 + [VMEM_SPEC] * 3,
        VMEM_SPEC,
        [pltpu.VMEM(LEFT_PANEL, lb.dtype)],
        FLOPS,
        8 * SLOTS_C * BLK * BLK,
    )(lw2, kw, lb2, right, total)
    return out[None, None]


def solution(mesh):
    in_specs = (
        P("row", "col", None, None, None),
        P("row", "col", None),
        P("row", "col", None, None, None),
        P("row", "col", None),
        P("row", "col", None),
    )
    out_specs = P("row", "col", None, None, None)
    return jax.shard_map(
        on_device, mesh=mesh, in_specs=in_specs, out_specs=out_specs, check_vma=False
    )
```

profile of v0, /device:TPU:32, one launch (start us, length us, event | category | flops | bytes accessed | tf_op | source)
XLA Modules:
  0.0 114.1 jit_solution(3333049725070522408)
XLA Ops:
  0.0 1.3 %collective-permute-start.20 = (bf16[32,128,128]{2,1,0:T(8,128)(2,1)}, bf16[32,128,128]{2,1,0:T(8,128)(2,1)S(1)}, u32[]{:S(2)}, u32[]{:S(2)}) collective-permute-start(bf16[32,128,128]{2,1,0:T(8,128)(2,1)} %bitcast.9), channel_id=1, source_target_pairs={{32,0},{33,1},{34,2},{35,3},{36,4},{37,5},{38,6},{39,7},{40,8},{41... | collective-permute-start | bytes 3145736 | tf_op jit(solution)/shard_map/ppermute | solution.py:172
  1.3 14.7 %collective-permute-start.16 = (s32[24]{0:T(128)}, s32[24]{0:T(128)S(1)}, u32[]{:S(2)}, u32[]{:S(2)}) collective-permute-start(s32[24]{0:T(128)} %bitcast.82), channel_id=1, source_target_pairs={{1,0},{2,1},{3,2},{4,3},{5,4},{6,5},{7,6},{8,7},{9,8},{10,9},{11,1... | collective-permute-start | bytes 296 | tf_op jit(solution)/shard_map/ppermute | solution.py:167
  16.0 13.1 %collective-permute-start.17 = (s32[32]{0:T(128)}, s32[32]{0:T(128)S(1)}, u32[]{:S(2)}, u32[]{:S(2)}) collective-permute-start(s32[32]{0:T(128)} %bitcast.63), channel_id=1, source_target_pairs={{64,32},{65,33},{66,34},{67,35},{68,36},{69,37},{70,38},{71,39},{7... | collective-permute-start | bytes 392 | tf_op jit(solution)/shard_map/ppermute | solution.py:168
  29.0 0.0 collective-permute-done.16.lw2.lw
  29.0 1.4 %collective-permute-done.17.rw2 = s32[32]{0:T(128)S(1)} collective-permute-done((s32[32]{0:T(128)}, s32[32]{0:T(128)S(1)}, u32[]{:S(2)}, u32[]{:S(2)}) %collective-permute-start.17) | collective-permute-done | bytes 160 | tf_op jit(solution)/shard_map/ppermute | solution.py:168
  30.4 8.1 %collective-permute-start.18 = (bf16[24,128,128]{2,1,0:T(8,128)(2,1)}, bf16[24,128,128]{2,1,0:T(8,128)(2,1)S(1)}, u32[]{:S(2)}, u32[]{:S(2)}) collective-permute-start(bf16[24,128,128]{2,1,0:T(8,128)(2,1)} %bitcast.27), channel_id=1, source_target_pairs={{1,0},{2,1},{3,2},{4,3},{5,4},{6,5},{7,6},{8,7},{9,8},{10,9},{11,1... | collective-permute-start | bytes 2359304 | tf_op jit(solution)/shard_map/ppermute | solution.py:171
  38.6 0.7 pad_add_fusion
  39.3 1.3 %collective-permute-start.19 = (s32[48]{0:T(128)S(1)}, s32[48]{0:T(128)S(1)}, u32[]{:S(2)}, u32[]{:S(2)}) collective-permute-start(s32[48]{0:T(128)S(1)} %pad_add_fusion), channel_id=1, source_target_pairs={{32,64},{33,65},{34,66},{35,67},{36,68},{37,69},{38,70},{39,71},{4... | collective-permute-start | bytes 584 | tf_op jit(solution)/shard_map/ppermute | solution.py:169
  40.6 14.4 %collective-permute-done.19.told = s32[48]{0:T(128)S(1)} collective-permute-done((s32[48]{0:T(128)S(1)}, s32[48]{0:T(128)S(1)}, u32[]{:S(2)}, u32[]{:S(2)}) %collective-permute-start.19) | collective-permute-done | bytes 224 | tf_op jit(solution)/shard_map/ppermute | solution.py:169
  55.0 2.9 %shard_map.55 = (s32[33]{0:T(128)S(1)}, bf16[32,128,128]{2,1,0:T(8,128)(2,1)S(1)}) custom-call(s32[1]{0:T(128)} %bitcast.4.across, s32[32]{0:T(128)} %bitcast.64, s32[32]{0:T(128)S(1)} %collective-permute-done.17.rw2, s32[24]{0:T(128)} %bitcast.45, s32[24]{0:T(128)S(1)} %collective-permute-done.16.lw2.lw, s32[48]{0:T(128)S(1)} %collective-permute-done.19.told, ...), custom_call_target="tpu_custom_call" | custom-call | bytes 1048576 | tf_op jit(solution)/shard_map/pallas_call | solution.py:174
  58.0 0.0 collective-permute-done.20
  58.0 52.1 %conditional.1 = (f32[24,128,128]{2,1,0:T(8,128)S(1)}, bf16[8,1152,128]{2,1,0:T(8,128)(2,1)S(1)}) conditional(s32[]{:T(128)} %clamp.3, (s32[24]{0:T(128)}, s32[32]{0:T(128)}, s32[24]{0:T(128)}, bf16[24,128,128]{2,1,0:T(8,128)(2,1)}, bf16[32,128,128]{2,1,0:T(8,128)(2,1)}, ...), branch_computations={%region_0.1_spmd, %region_1.2_spmd, %region_2.3_spmd, %region_3.4_... | conditional | flops 805306368 | bytes 15861188 | solution.py:218
  58.0 0.0 copy-start.3
  58.0 0.0 copy-start.9
  58.1 0.0 copy-start.13
  58.1 0.0 copy-start.17
  58.1 0.1 slice.43
  58.1 1.5 %collective-permute-start.11 = (bf16[24,128,128]{2,1,0:T(8,128)(2,1)S(1)}, bf16[24,128,128]{2,1,0:T(8,128)(2,1)S(1)}, u32[]{:S(2)}, u32[]{:S(2)}) collective-permute-start(bf16[24,128,128]{2,1,0:T(8,128)(2,1)S(1)} %slice.43), channel_id=1, source_target_pairs={{64,32},{65,33},{66,34},{67,35},{68,36},{69,37},{70,38},{71,39},{7... | collective-permute-start | bytes 2359304 | tf_op jit(solution)/shard_map/cond/branch_11_fun/ppermute | solution.py:193
  59.6 0.0 copy-done.3
  59.6 0.0 copy-done.9
  59.6 0.0 copy-done.13
  59.7 0.0 copy-done.17
  59.7 7.4 %branch_11_fun.2 = f32[24,128,128]{2,1,0:T(8,128)S(1)} custom-call(s32[24]{0:T(128)S(1)} %copy-done.17, s32[32]{0:T(128)S(1)} %copy-done.13, s32[24]{0:T(128)S(1)} %copy-done.9, bf16[24,128,128]{2,1,0:T(8,128)(2,1)} %get-tuple-element.438.left_blocks, bf16[32,128,128]{2,1,0:T(8,128)(2,1)S(1)} %copy-done.3), custom_call_target="tpu_custom_call" | custom-call | flops 805306368 | bytes 1572864 | tf_op jit(solution)/shard_map/cond/branch_11_fun/pallas_call | solution.py:194
  67.1 41.8 %collective-permute-done.11.arrived = bf16[24,128,128]{2,1,0:T(8,128)(2,1)S(1)} collective-permute-done((bf16[24,128,128]{2,1,0:T(8,128)(2,1)S(1)}, bf16[24,128,128]{2,1,0:T(8,128)(2,1)S(1)}, u32[]{:S(2)}, u32[]{:S(2)}) %collective-permute-start.11) | collective-permute-done | bytes 786464 | tf_op jit(solution)/shard_map/cond/branch_11_fun/ppermute | solution.py:193
  108.9 1.1 %branch_11_fun.3 = bf16[8,1152,128]{2,1,0:T(8,128)(2,1)S(1)} custom-call(s32[1]{0:T(128)} %get-tuple-element.440.across, s32[33]{0:T(128)S(1)} %get-tuple-element.441.meta, s32[32]{0:T(128)S(1)} %get-tuple-element.442.rw, bf16[24,128,128]{2,1,0:T(8,128)(2,1)S(1)} %collective-permute-done.11.arrived, bf16[32,128,128]{2,1,0:T(8,128)(2,1)S(1)} %get-tuple-element.444.beside), custom_call_target="tpu_custom_call" | custom-call | bytes 1048576 | tf_op jit(solution)/shard_map/cond/branch_11_fun/pallas_call | solution.py:203
  110.1 0.0 collective-permute-done.18.left_blocks
  110.1 4.0 %shard_map.56 = f32[24,128,128]{2,1,0:T(8,128)} custom-call(s32[24]{0:T(128)S(1)} %collective-permute-done.16.lw2.lw, s32[24]{0:T(128)} %bitcast.62, bf16[24,128,128]{2,1,0:T(8,128)(2,1)S(1)} %collective-permute-done.18.left_blocks, bf16[8,1152,128]{2,1,0:T(8,128)(2,1)S(1)} %get-tuple-element.493.right, f32[24,128,128]{2,1,0:T(8,128)S(1)} %get-tuple-element.494.total), custom_call_target="tpu_custom_call" | custom-call | flops 805306368 | bytes 3145728 | tf_op jit(solution)/shard_map/pallas_call | solution.py:223
Async XLA Ops:
  0.0 58.0 %collective-permute-start.20 = (bf16[32,128,128]{2,1,0:T(8,128)(2,1)}, bf16[32,128,128]{2,1,0:T(8,128)(2,1)S(1)}, u32[]{:S(2)}, u32[]{:S(2)}) collective-permute-start(bf16[32,128,128]{2,1,0:T(8,128)(2,1)} %bitcast.9), channel_id=1, source_target_pairs={{32,0},{33,1},{34,2},{35,3},{36,4},{37,5},{38,6},{39,7},{40,8},{41... | collective-permute-start | bytes 3145736 | tf_op jit(solution)/shard_map/ppermute | solution.py:172
  1.3 27.7 %collective-permute-start.16 = (s32[24]{0:T(128)}, s32[24]{0:T(128)S(1)}, u32[]{:S(2)}, u32[]{:S(2)}) collective-permute-start(s32[24]{0:T(128)} %bitcast.82), channel_id=1, source_target_pairs={{1,0},{2,1},{3,2},{4,3},{5,4},{6,5},{7,6},{8,7},{9,8},{10,9},{11,1... | collective-permute-start | bytes 296 | tf_op jit(solution)/shard_map/ppermute | solution.py:167
  16.0 14.5 %collective-permute-start.17 = (s32[32]{0:T(128)}, s32[32]{0:T(128)S(1)}, u32[]{:S(2)}, u32[]{:S(2)}) collective-permute-start(s32[32]{0:T(128)} %bitcast.63), channel_id=1, source_target_pairs={{64,32},{65,33},{66,34},{67,35},{68,36},{69,37},{70,38},{71,39},{7... | collective-permute-start | bytes 392 | tf_op jit(solution)/shard_map/ppermute | solution.py:168
  30.4 79.6 %collective-permute-start.18 = (bf16[24,128,128]{2,1,0:T(8,128)(2,1)}, bf16[24,128,128]{2,1,0:T(8,128)(2,1)S(1)}, u32[]{:S(2)}, u32[]{:S(2)}) collective-permute-start(bf16[24,128,128]{2,1,0:T(8,128)(2,1)} %bitcast.27), channel_id=1, source_target_pairs={{1,0},{2,1},{3,2},{4,3},{5,4},{6,5},{7,6},{8,7},{9,8},{10,9},{11,1... | collective-permute-start | bytes 2359304 | tf_op jit(solution)/shard_map/ppermute | solution.py:171
  39.3 15.7 %collective-permute-start.19 = (s32[48]{0:T(128)S(1)}, s32[48]{0:T(128)S(1)}, u32[]{:S(2)}, u32[]{:S(2)}) collective-permute-start(s32[48]{0:T(128)S(1)} %pad_add_fusion), channel_id=1, source_target_pairs={{32,64},{33,65},{34,66},{35,67},{36,68},{37,69},{38,70},{39,71},{4... | collective-permute-start | bytes 584 | tf_op jit(solution)/shard_map/ppermute | solution.py:169
  58.0 1.6 %copy-start.3 = (bf16[32,128,128]{2,1,0:T(8,128)(2,1)S(1)}, bf16[32,128,128]{2,1,0:T(8,128)(2,1)}, u32[]{:S(2)}) copy-start(bf16[32,128,128]{2,1,0:T(8,128)(2,1)} %get-tuple-element.439.right_blocks) | copy-start | bytes 3145732 | tf_op jit(solution)/shard_map/cond
  58.0 1.6 %copy-start.9 = (s32[24]{0:T(128)S(1)}, s32[24]{0:T(128)}, u32[]{:S(2)}) copy-start(s32[24]{0:T(128)} %get-tuple-element.437.kw) | copy-start | bytes 292 | tf_op jit(solution)/shard_map/cond
  58.1 1.6 %copy-start.13 = (s32[32]{0:T(128)S(1)}, s32[32]{0:T(128)}, u32[]{:S(2)}) copy-start(s32[32]{0:T(128)} %get-tuple-element.436.rw) | copy-start | bytes 388 | tf_op jit(solution)/shard_map/cond
  58.1 1.6 %copy-start.17 = (s32[24]{0:T(128)S(1)}, s32[24]{0:T(128)}, u32[]{:S(2)}) copy-start(s32[24]{0:T(128)} %get-tuple-element.435.lw) | copy-start | bytes 292 | tf_op jit(solution)/shard_map/cond
  58.1 50.8 %collective-permute-start.11 = (bf16[24,128,128]{2,1,0:T(8,128)(2,1)S(1)}, bf16[24,128,128]{2,1,0:T(8,128)(2,1)S(1)}, u32[]{:S(2)}, u32[]{:S(2)}) collective-permute-start(bf16[24,128,128]{2,1,0:T(8,128)(2,1)S(1)} %slice.43), channel_id=1, source_target_pairs={{64,32},{65,33},{66,34},{67,35},{68,36},{69,37},{70,38},{71,39},{7... | collective-permute-start | bytes 2359304 | tf_op jit(solution)/shard_map/cond/branch_11_fun/ppermute | solution.py:193
where the time goes:
time: 114 us
  waiting for transfers between devices  57.7 us (51%)
  starting transfers between devices  39.9 us (35%)
  Pallas kernels  15.4 us (14%)
    ppermute x1, waiting for transfers between devices, body(): arrived = lax.ppermute(packed[:size], AXES, across)  41.8 us
    ppermute x1, starting transfers between devices, on_device(): lw2 = lax.ppermute(lw, AXES, left_on)  14.7 us
    ppermute x1, waiting for transfers between devices, on_device(): told = lax.ppermute(jnp.concatenate([kw, lw2]), AXES, back)  14.4 us
    ppermute x1, starting transfers between devices, on_device(): rw2 = lax.ppermute(rw, AXES, across + beside)  13.1 us
    ppermute x1, starting transfers between devices, on_device(): lb2 = lax.ppermute(lb_sent, AXES, left_on)  8.1 us
    pallas_call x1, Pallas kernels, body(): call(own_kernel, jax.ShapeDtypeStruct((SLOTS_C, BLK, BLK), jnp.float32),...  7.39 us
    pallas_call x1, Pallas kernels, on_device(): call(last_kernel, jax.ShapeDtypeStruct((SLOTS_C, BLK, BLK), jnp.float32),...  4 us
    pallas_call x1, Pallas kernels, on_device(): call(plan_kernel, (jax.ShapeDtypeStruct((SLOTS_B + 1,), jnp.int32), jax.S...  2.89 us
  transfers between devices with their start and end apart: 6, of which 3 were waited for; matrix products, arithmetic and copies ran while one was open for 1% of the time, Pallas kernels for 10%

commit v1 on v0

--- a/solution.py
+++ b/solution.py
@@ -12,7 +12,7 @@
 SLOTS_A = 24
 SLOTS_B = 32
 SLOTS_C = 24
-STEP = 2
+STEP = 1
 AXES = ("row", "col")
 VMEM_LIMIT = 40 * 1024 * 1024
 

time: 114 us -> 117 us (1.026)
  the two profiles are of different devices: /device:TPU:32 before, /device:TPU:28 now
where the time goes in v1:
time: 117 us; the launch traced here: 115 us
  waiting for transfers between devices  62.3 us (53%)
  starting transfers between devices  36.2 us (31%)
  Pallas kernels  15.4 us (13%)
    ppermute x1, waiting for transfers between devices, body(): arrived = lax.ppermute(packed[:size], AXES, across)  37.8 us
    ppermute x1, waiting for transfers between devices, on_device(): told = lax.ppermute(jnp.concatenate([kw, lw2]), AXES, back)  23.1 us
    ppermute x1, starting transfers between devices, on_device(): rw2 = lax.ppermute(rw, AXES, across + beside)  16 us
    ppermute x1, starting transfers between devices, on_device(): lw2 = lax.ppermute(lw, AXES, left_on)  13.3 us
    pallas_call x1, Pallas kernels, body(): call(own_kernel, jax.ShapeDtypeStruct((SLOTS_C, BLK, BLK), jnp.float32),...  7.39 us
    pallas_call x1, Pallas kernels, on_device(): call(last_kernel, jax.ShapeDtypeStruct((SLOTS_C, BLK, BLK), jnp.float32),...  4 us
    ppermute x1, starting transfers between devices, on_device(): lb2 = lax.ppermute(lb_sent, AXES, left_on)  2.91 us
    pallas_call x1, Pallas kernels, on_device(): call(plan_kernel, (jax.ShapeDtypeStruct((SLOTS_B + 1,), jnp.int32), jax.S...  2.84 us
  transfers between devices with their start and end apart: 6, of which 3 were waited for; matrix products, arithmetic and copies ran while one was open for 1% of the time, Pallas kernels for 10%

profile of v1, /device:TPU:28, one launch (start us, length us, event | category | flops | bytes accessed | tf_op | source)
XLA Modules:
  0.0 115.4 jit_solution(1255541812231286213)
XLA Ops:
  0.0 1.3 %collective-permute-start.36 = (bf16[32,128,128]{2,1,0:T(8,128)(2,1)}, bf16[32,128,128]{2,1,0:T(8,128)(2,1)S(1)}, u32[]{:S(2)}, u32[]{:S(2)}) collective-permute-start(bf16[32,128,128]{2,1,0:T(8,128)(2,1)} %bitcast.9), channel_id=1, source_target_pairs={{32,0},{33,1},{34,2},{35,3},{36,4},{37,5},{38,6},{39,7},{40,8},{41... | collective-permute-start | bytes 3145736 | tf_op jit(solution)/shard_map/ppermute | solution.py:172
  1.3 13.3 %collective-permute-start.32 = (s32[24]{0:T(128)}, s32[24]{0:T(128)S(1)}, u32[]{:S(2)}, u32[]{:S(2)}) collective-permute-start(s32[24]{0:T(128)} %bitcast.146), channel_id=1, source_target_pairs={{1,0},{2,1},{3,2},{4,3},{5,4},{6,5},{7,6},{8,7},{9,8},{10,9},{11,1... | collective-permute-start | bytes 296 | tf_op jit(solution)/shard_map/ppermute | solution.py:167
  14.6 16.0 %collective-permute-start.33 = (s32[32]{0:T(128)}, s32[32]{0:T(128)S(1)}, u32[]{:S(2)}, u32[]{:S(2)}) collective-permute-start(s32[32]{0:T(128)} %bitcast.111), channel_id=1, source_target_pairs={{64,32},{65,33},{66,34},{67,35},{68,36},{69,37},{70,38},{71,39},{7... | collective-permute-start | bytes 392 | tf_op jit(solution)/shard_map/ppermute | solution.py:168
  30.6 0.0 collective-permute-done.32.lw2.lw
  30.6 1.4 %collective-permute-done.33.rw2 = s32[32]{0:T(128)S(1)} collective-permute-done((s32[32]{0:T(128)}, s32[32]{0:T(128)S(1)}, u32[]{:S(2)}, u32[]{:S(2)}) %collective-permute-start.33) | collective-permute-done | bytes 160 | tf_op jit(solution)/shard_map/ppermute | solution.py:168
  32.0 2.9 %collective-permute-start.34 = (bf16[24,128,128]{2,1,0:T(8,128)(2,1)}, bf16[24,128,128]{2,1,0:T(8,128)(2,1)S(1)}, u32[]{:S(2)}, u32[]{:S(2)}) collective-permute-start(bf16[24,128,128]{2,1,0:T(8,128)(2,1)} %bitcast.43), channel_id=1, source_target_pairs={{1,0},{2,1},{3,2},{4,3},{5,4},{6,5},{7,6},{8,7},{9,8},{10,9},{11,1... | collective-permute-start | bytes 2359304 | tf_op jit(solution)/shard_map/ppermute | solution.py:171
  35.0 0.7 pad_add_fusion
  35.7 1.3 %collective-permute-start.35 = (s32[48]{0:T(128)S(1)}, s32[48]{0:T(128)S(1)}, u32[]{:S(2)}, u32[]{:S(2)}) collective-permute-start(s32[48]{0:T(128)S(1)} %pad_add_fusion), channel_id=1, source_target_pairs={{32,64},{33,65},{34,66},{35,67},{36,68},{37,69},{38,70},{39,71},{4... | collective-permute-start | bytes 584 | tf_op jit(solution)/shard_map/ppermute | solution.py:169
  37.0 23.1 %collective-permute-done.35.told = s32[48]{0:T(128)S(1)} collective-permute-done((s32[48]{0:T(128)S(1)}, s32[48]{0:T(128)S(1)}, u32[]{:S(2)}, u32[]{:S(2)}) %collective-permute-start.35) | collective-permute-done | bytes 224 | tf_op jit(solution)/shard_map/ppermute | solution.py:169
  60.1 2.8 %shard_map.55 = (s32[33]{0:T(128)S(1)}, bf16[32,128,128]{2,1,0:T(8,128)(2,1)S(1)}) custom-call(s32[1]{0:T(128)} %bitcast.4.across, s32[32]{0:T(128)} %bitcast.112, s32[32]{0:T(128)S(1)} %collective-permute-done.33.rw2, s32[24]{0:T(128)} %bitcast.77, s32[24]{0:T(128)S(1)} %collective-permute-done.32.lw2.lw, s32[48]{0:T(128)S(1)} %collective-permute-done.35.told, ...), custom_call_target="tpu_custom_call" | custom-call | bytes 1048576 | tf_op jit(solution)/shard_map/pallas_call | solution.py:174
  63.0 0.0 collective-permute-done.36
  63.0 48.4 %conditional.1 = (f32[24,128,128]{2,1,0:T(8,128)S(1)}, bf16[8,1152,128]{2,1,0:T(8,128)(2,1)S(1)}) conditional(s32[]{:T(128)} %bitcast.6, (s32[24]{0:T(128)}, s32[32]{0:T(128)}, s32[24]{0:T(128)}, bf16[24,128,128]{2,1,0:T(8,128)(2,1)}, bf16[32,128,128]{2,1,0:T(8,128)(2,1)}, ...), branch_computations={%region_0.1_spmd, %region_1.2_spmd, %region_2.3_spmd, %region_3.4_... | conditional | flops 805306368 | bytes 16057796 | solution.py:218
  63.0 0.0 copy-start
  63.1 1.5 %collective-permute-start.17 = (bf16[18,128,128]{2,1,0:T(8,128)(2,1)S(1)}, bf16[18,128,128]{2,1,0:T(8,128)(2,1)S(1)}, u32[]{:S(2)}, u32[]{:S(2)}) collective-permute-start(bf16[18,128,128]{2,1,0:T(8,128)(2,1)S(1)} %slice.81), channel_id=1, source_target_pairs={{64,32},{65,33},{66,34},{67,35},{68,36},{69,37},{70,38},{71,39},{7... | collective-permute-start | bytes 1769480 | tf_op jit(solution)/shard_map/cond/branch_17_fun/ppermute | solution.py:193
  64.6 0.0 copy-done
  64.6 7.4 %branch_17_fun.2 = f32[24,128,128]{2,1,0:T(8,128)S(1)} custom-call(s32[24]{0:T(128)} %get-tuple-element.815.lw, s32[32]{0:T(128)} %get-tuple-element.816.rw, s32[24]{0:T(128)} %get-tuple-element.817.kw, bf16[24,128,128]{2,1,0:T(8,128)(2,1)} %get-tuple-element.818.left_blocks, bf16[32,128,128]{2,1,0:T(8,128)(2,1)S(1)} %copy-done), custom_call_target="tpu_custom_call" | custom-call | flops 805306368 | bytes 1572864 | tf_op jit(solution)/shard_map/cond/branch_17_fun/pallas_call | solution.py:194
  72.0 37.8 %collective-permute-done.17.arrived = bf16[18,128,128]{2,1,0:T(8,128)(2,1)S(1)} collective-permute-done((bf16[18,128,128]{2,1,0:T(8,128)(2,1)S(1)}, bf16[18,128,128]{2,1,0:T(8,128)(2,1)S(1)}, u32[]{:S(2)}, u32[]{:S(2)}) %collective-permute-start.17) | collective-permute-done | bytes 589856 | tf_op jit(solution)/shard_map/cond/branch_17_fun/ppermute | solution.py:193
  109.8 1.1 branch_17_fun.3
  111.4 0.0 collective-permute-done.34.left_blocks
  111.4 4.0 %shard_map.56 = f32[24,128,128]{2,1,0:T(8,128)} custom-call(s32[24]{0:T(128)S(1)} %collective-permute-done.32.lw2.lw, s32[24]{0:T(128)} %bitcast.110, bf16[24,128,128]{2,1,0:T(8,128)(2,1)S(1)} %collective-permute-done.34.left_blocks, bf16[8,1152,128]{2,1,0:T(8,128)(2,1)S(1)} %get-tuple-element.973.right, f32[24,128,128]{2,1,0:T(8,128)S(1)} %get-tuple-element.974.total), custom_call_target="tpu_custom_call" | custom-call | flops 805306368 | bytes 3145728 | tf_op jit(solution)/shard_map/pallas_call | solution.py:223
  (1 shorter events, 0.0 us)
Async XLA Ops:
  0.0 63.0 %collective-permute-start.36 = (bf16[32,128,128]{2,1,0:T(8,128)(2,1)}, bf16[32,128,128]{2,1,0:T(8,128)(2,1)S(1)}, u32[]{:S(2)}, u32[]{:S(2)}) collective-permute-start(bf16[32,128,128]{2,1,0:T(8,128)(2,1)} %bitcast.9), channel_id=1, source_target_pairs={{32,0},{33,1},{34,2},{35,3},{36,4},{37,5},{38,6},{39,7},{40,8},{41... | collective-permute-start | bytes 3145736 | tf_op jit(solution)/shard_map/ppermute | solution.py:172
  1.3 29.3 %collective-permute-start.32 = (s32[24]{0:T(128)}, s32[24]{0:T(128)S(1)}, u32[]{:S(2)}, u32[]{:S(2)}) collective-permute-start(s32[24]{0:T(128)} %bitcast.146), channel_id=1, source_target_pairs={{1,0},{2,1},{3,2},{4,3},{5,4},{6,5},{7,6},{8,7},{9,8},{10,9},{11,1... | collective-permute-start | bytes 296 | tf_op jit(solution)/shard_map/ppermute | solution.py:167
  14.6 17.4 %collective-permute-start.33 = (s32[32]{0:T(128)}, s32[32]{0:T(128)S(1)}, u32[]{:S(2)}, u32[]{:S(2)}) collective-permute-start(s32[32]{0:T(128)} %bitcast.111), channel_id=1, source_target_pairs={{64,32},{65,33},{66,34},{67,35},{68,36},{69,37},{70,38},{71,39},{7... | collective-permute-start | bytes 392 | tf_op jit(solution)/shard_map/ppermute | solution.py:168
  32.0 79.3 %collective-permute-start.34 = (bf16[24,128,128]{2,1,0:T(8,128)(2,1)}, bf16[24,128,128]{2,1,0:T(8,128)(2,1)S(1)}, u32[]{:S(2)}, u32[]{:S(2)}) collective-permute-start(bf16[24,128,128]{2,1,0:T(8,128)(2,1)} %bitcast.43), channel_id=1, source_target_pairs={{1,0},{2,1},{3,2},{4,3},{5,4},{6,5},{7,6},{8,7},{9,8},{10,9},{11,1... | collective-permute-start | bytes 2359304 | tf_op jit(solution)/shard_map/ppermute | solution.py:171
  35.7 24.4 %collective-permute-start.35 = (s32[48]{0:T(128)S(1)}, s32[48]{0:T(128)S(1)}, u32[]{:S(2)}, u32[]{:S(2)}) collective-permute-start(s32[48]{0:T(128)S(1)} %pad_add_fusion), channel_id=1, source_target_pairs={{32,64},{33,65},{34,66},{35,67},{36,68},{37,69},{38,70},{39,71},{4... | collective-permute-start | bytes 584 | tf_op jit(solution)/shard_map/ppermute | solution.py:169
  63.0 1.5 %copy-start = (bf16[32,128,128]{2,1,0:T(8,128)(2,1)S(1)}, bf16[32,128,128]{2,1,0:T(8,128)(2,1)}, u32[]{:S(2)}) copy-start(bf16[32,128,128]{2,1,0:T(8,128)(2,1)} %get-tuple-element.819.right_blocks) | copy-start | bytes 3145732 | tf_op jit(solution)/shard_map/cond
  63.1 46.7 %collective-permute-start.17 = (bf16[18,128,128]{2,1,0:T(8,128)(2,1)S(1)}, bf16[18,128,128]{2,1,0:T(8,128)(2,1)S(1)}, u32[]{:S(2)}, u32[]{:S(2)}) collective-permute-start(bf16[18,128,128]{2,1,0:T(8,128)(2,1)S(1)} %slice.81), channel_id=1, source_target_pairs={{64,32},{65,33},{66,34},{67,35},{68,36},{69,37},{70,38},{71,39},{7... | collective-permute-start | bytes 1769480 | tf_op jit(solution)/shard_map/cond/branch_17_fun/ppermute | solution.py:193

commit v2 on v1

--- a/solution.py
+++ b/solution.py
@@ -125,10 +125,17 @@
         fill_right(right, lambda s: meta[1 + s], arrived, meta[0])
 
 
-def last_kernel(lw, kw, left_blocks, right, total, out, left):
+def last_kernel(lw, kw, left_blocks, right, total, out, left, ready, sems):
     fill_left(left, lw, left_blocks)
+
+    def copy(u):
+        return pltpu.make_async_copy(ready.at[u], out.at[u], sems.at[u])
+
     for u in range(SLOTS_C):
-        out[u] = total[u] + block_product(left, right, kw[u])
+        ready[u] = total[u] + block_product(left, right, kw[u])
+        copy(u).start()
+    for u in range(SLOTS_C):
+        copy(u).wait()
 
 
 def call(kernel, out_shape, in_specs, out_specs, scratch, flops, moved):
@@ -166,10 +173,13 @@
 
     lw2 = lax.ppermute(lw, AXES, left_on)
     rw2 = lax.ppermute(rw, AXES, across + beside)
-    told = lax.ppermute(jnp.concatenate([kw, lw2]), AXES, back)
+    note = jnp.concatenate([kw, lw2])
+    note, rw2 = lax.optimization_barrier((note, rw2))
+    told = lax.ppermute(note, AXES, back)
     lb_sent, _ = lax.optimization_barrier((lb, (lw2, rw2)))
     lb2 = lax.ppermute(lb_sent, AXES, left_on)
-    beside_blocks = lax.ppermute(rb, AXES, beside)
+    rb_sent, _ = lax.optimization_barrier((rb, note))
+    beside_blocks = lax.ppermute(rb_sent, AXES, beside)
 
     meta, packed = call(
         plan_kernel,
@@ -224,8 +234,12 @@
         last_kernel,
         jax.ShapeDtypeStruct((SLOTS_C, BLK, BLK), jnp.float32),
         [SMEM_SPEC] * 2 + [VMEM_SPEC] * 3,
-        VMEM_SPEC,
-        [pltpu.VMEM(LEFT_PANEL, lb.dtype)],
+        ANY_SPEC,
+        [
+            pltpu.VMEM(LEFT_PANEL, lb.dtype),
+            pltpu.VMEM((SLOTS_C, BLK, BLK), jnp.float32),
+            pltpu.SemaphoreType.DMA((SLOTS_C,)),
+        ],
         FLOPS,
         8 * SLOTS_C * BLK * BLK,
     )(lw2, kw, lb2, right, total)

time: 117 us -> 116 us (level)
  the two profiles are of different devices: /device:TPU:28 before, /device:TPU:32 now
where the time goes in v2:
time: 116 us; the launch traced here: 115 us
  waiting for transfers between devices  60 us (52%)
  starting transfers between devices  38.5 us (33%)
  Pallas kernels  15.1 us (13%)
    ppermute x1, waiting for transfers between devices, body(): arrived = lax.ppermute(packed[:size], AXES, across)  44.8 us
    ppermute x1, starting transfers between devices, on_device(): lw2 = lax.ppermute(lw, AXES, left_on)  14.7 us
    ppermute x1, waiting for transfers between devices, on_device(): told = lax.ppermute(note, AXES, back)  14.4 us
    ppermute x1, starting transfers between devices, on_device(): rw2 = lax.ppermute(rw, AXES, across + beside)  11.7 us
    ppermute x1, starting transfers between devices, on_device(): lb2 = lax.ppermute(lb_sent, AXES, left_on)  8.11 us
    pallas_call x1, Pallas kernels, body(): call(own_kernel, jax.ShapeDtypeStruct((SLOTS_C, BLK, BLK), jnp.float32),...  7.39 us
    pallas_call x1, Pallas kernels, on_device(): call(last_kernel, jax.ShapeDtypeStruct((SLOTS_C, BLK, BLK), jnp.float32),...  3.7 us
    pallas_call x1, Pallas kernels, on_device(): call(plan_kernel, (jax.ShapeDtypeStruct((SLOTS_B + 1,), jnp.int32), jax.S...  2.88 us
  transfers between devices with their start and end apart: 6, of which 3 were waited for; matrix products, arithmetic and copies ran while one was open for 1% of the time, Pallas kernels for 10%

profile of v2, /device:TPU:32, one launch (start us, length us, event | category | flops | bytes accessed | tf_op | source)
XLA Modules:
  0.0 115.2 jit_solution(16730696363778999227)
XLA Ops:
  0.0 14.7 %collective-permute-start.32 = (s32[24]{0:T(128)}, s32[24]{0:T(128)S(1)}, u32[]{:S(2)}, u32[]{:S(2)}) collective-permute-start(s32[24]{0:T(128)} %bitcast.146), channel_id=1, source_target_pairs={{1,0},{2,1},{3,2},{4,3},{5,4},{6,5},{7,6},{8,7},{9,8},{10,9},{11,1... | collective-permute-start | bytes 296 | tf_op jit(solution)/shard_map/ppermute | solution.py:174
  14.7 11.7 %collective-permute-start.33 = (s32[32]{0:T(128)}, s32[32]{0:T(128)S(1)}, u32[]{:S(2)}, u32[]{:S(2)}) collective-permute-start(s32[32]{0:T(128)} %bitcast.111), channel_id=1, source_target_pairs={{64,32},{65,33},{66,34},{67,35},{68,36},{69,37},{70,38},{71,39},{7... | collective-permute-start | bytes 392 | tf_op jit(solution)/shard_map/ppermute | solution.py:175
  26.4 0.0 collective-permute-done.32.lw2.lw
  26.4 0.7 pad_add_fusion
  27.1 0.7 collective-permute-done.33.rw2
  27.8 1.3 %collective-permute-start.36 = (bf16[32,128,128]{2,1,0:T(8,128)(2,1)}, bf16[32,128,128]{2,1,0:T(8,128)(2,1)S(1)}, u32[]{:S(2)}, u32[]{:S(2)}) collective-permute-start(bf16[32,128,128]{2,1,0:T(8,128)(2,1)} %bitcast.9), channel_id=1, source_target_pairs={{32,0},{33,1},{34,2},{35,3},{36,4},{37,5},{38,6},{39,7},{40,8},{41... | collective-permute-start | bytes 3145736 | tf_op jit(solution)/shard_map/ppermute | solution.py:182
  29.1 8.1 %collective-permute-start.34 = (bf16[24,128,128]{2,1,0:T(8,128)(2,1)}, bf16[24,128,128]{2,1,0:T(8,128)(2,1)S(1)}, u32[]{:S(2)}, u32[]{:S(2)}) collective-permute-start(bf16[24,128,128]{2,1,0:T(8,128)(2,1)} %bitcast.43), channel_id=1, source_target_pairs={{1,0},{2,1},{3,2},{4,3},{5,4},{6,5},{7,6},{8,7},{9,8},{10,9},{11,1... | collective-permute-start | bytes 2359304 | tf_op jit(solution)/shard_map/ppermute | solution.py:180
  37.2 1.3 %collective-permute-start.35 = (s32[48]{0:T(128)S(1)}, s32[48]{0:T(128)S(1)}, u32[]{:S(2)}, u32[]{:S(2)}) collective-permute-start(s32[48]{0:T(128)S(1)} %pad_add_fusion), channel_id=1, source_target_pairs={{32,64},{33,65},{34,66},{35,67},{36,68},{37,69},{38,70},{39,71},{4... | collective-permute-start | bytes 584 | tf_op jit(solution)/shard_map/ppermute | solution.py:178
  38.5 14.4 %collective-permute-done.35.told = s32[48]{0:T(128)S(1)} collective-permute-done((s32[48]{0:T(128)S(1)}, s32[48]{0:T(128)S(1)}, u32[]{:S(2)}, u32[]{:S(2)}) %collective-permute-start.35) | collective-permute-done | bytes 224 | tf_op jit(solution)/shard_map/ppermute | solution.py:178
  52.9 2.9 %shard_map.55 = (s32[33]{0:T(128)S(1)}, bf16[32,128,128]{2,1,0:T(8,128)(2,1)S(1)}) custom-call(s32[1]{0:T(128)} %bitcast.4.across, s32[32]{0:T(128)} %bitcast.112, s32[32]{0:T(128)S(1)} %collective-permute-done.33.rw2, s32[24]{0:T(128)} %bitcast.77, s32[24]{0:T(128)S(1)} %collective-permute-done.32.lw2.lw, s32[48]{0:T(128)S(1)} %collective-permute-done.35.told, ...), custom_call_target="tpu_custom_call" | custom-call | bytes 1048576 | tf_op jit(solution)/shard_map/pallas_call | solution.py:184
  55.9 0.0 collective-permute-done.36
  55.9 55.4 %conditional.1 = (f32[24,128,128]{2,1,0:T(8,128)S(1)}, bf16[8,1152,128]{2,1,0:T(8,128)(2,1)S(1)}) conditional(s32[]{:T(128)} %bitcast.6, (s32[24]{0:T(128)}, s32[32]{0:T(128)}, s32[24]{0:T(128)}, bf16[24,128,128]{2,1,0:T(8,128)(2,1)}, bf16[32,128,128]{2,1,0:T(8,128)(2,1)}, ...), branch_computations={%region_0.1_spmd, %region_1.2_spmd, %region_2.3_spmd, %region_3.4_... | conditional | flops 805306368 | bytes 16057796 | solution.py:228
  55.9 0.0 copy-start.4
  55.9 0.1 slice.85
  56.0 1.5 %collective-permute-start.21 = (bf16[22,128,128]{2,1,0:T(8,128)(2,1)S(1)}, bf16[22,128,128]{2,1,0:T(8,128)(2,1)S(1)}, u32[]{:S(2)}, u32[]{:S(2)}) collective-permute-start(bf16[22,128,128]{2,1,0:T(8,128)(2,1)S(1)} %slice.85), channel_id=1, source_target_pairs={{64,32},{65,33},{66,34},{67,35},{68,36},{69,37},{70,38},{71,39},{7... | collective-permute-start | bytes 2162696 | tf_op jit(solution)/shard_map/cond/branch_21_fun/ppermute | solution.py:203
  57.5 0.0 copy-done.4
  57.5 7.4 %branch_21_fun.2 = f32[24,128,128]{2,1,0:T(8,128)S(1)} custom-call(s32[24]{0:T(128)} %get-tuple-element.855.lw, s32[32]{0:T(128)} %get-tuple-element.856.rw, s32[24]{0:T(128)} %get-tuple-element.857.kw, bf16[24,128,128]{2,1,0:T(8,128)(2,1)} %get-tuple-element.858.left_blocks, bf16[32,128,128]{2,1,0:T(8,128)(2,1)S(1)} %copy-done.4), custom_call_target="tpu_custom_call" | custom-call | flops 805306368 | bytes 1572864 | tf_op jit(solution)/shard_map/cond/branch_21_fun/pallas_call | solution.py:204
  64.9 44.8 %collective-permute-done.21.arrived = bf16[22,128,128]{2,1,0:T(8,128)(2,1)S(1)} collective-permute-done((bf16[22,128,128]{2,1,0:T(8,128)(2,1)S(1)}, bf16[22,128,128]{2,1,0:T(8,128)(2,1)S(1)}, u32[]{:S(2)}, u32[]{:S(2)}) %collective-permute-start.21) | collective-permute-done | bytes 720928 | tf_op jit(solution)/shard_map/cond/branch_21_fun/ppermute | solution.py:203
  109.7 1.1 branch_21_fun.3
  111.3 0.0 collective-permute-done.34.left_blocks
  111.3 3.7 %shard_map.56 = f32[24,128,128]{2,1,0:T(8,128)} custom-call(s32[24]{0:T(128)S(1)} %collective-permute-done.32.lw2.lw, s32[24]{0:T(128)} %bitcast.110, bf16[24,128,128]{2,1,0:T(8,128)(2,1)S(1)} %collective-permute-done.34.left_blocks, bf16[8,1152,128]{2,1,0:T(8,128)(2,1)S(1)} %get-tuple-element.979.right, f32[24,128,128]{2,1,0:T(8,128)S(1)} %get-tuple-element.980.total), custom_call_target="tpu_custom_call" | custom-call | flops 805306368 | bytes 3145728 | tf_op jit(solution)/shard_map/pallas_call | solution.py:233
Async XLA Ops:
  0.0 26.4 %collective-permute-start.32 = (s32[24]{0:T(128)}, s32[24]{0:T(128)S(1)}, u32[]{:S(2)}, u32[]{:S(2)}) collective-permute-start(s32[24]{0:T(128)} %bitcast.146), channel_id=1, source_target_pairs={{1,0},{2,1},{3,2},{4,3},{5,4},{6,5},{7,6},{8,7},{9,8},{10,9},{11,1... | collective-permute-start | bytes 296 | tf_op jit(solution)/shard_map/ppermute | solution.py:174
  14.7 13.1 %collective-permute-start.33 = (s32[32]{0:T(128)}, s32[32]{0:T(128)S(1)}, u32[]{:S(2)}, u32[]{:S(2)}) collective-permute-start(s32[32]{0:T(128)} %bitcast.111), channel_id=1, source_target_pairs={{64,32},{65,33},{66,34},{67,35},{68,36},{69,37},{70,38},{71,39},{7... | collective-permute-start | bytes 392 | tf_op jit(solution)/shard_map/ppermute | solution.py:175
  27.8 28.1 %collective-permute-start.36 = (bf16[32,128,128]{2,1,0:T(8,128)(2,1)}, bf16[32,128,128]{2,1,0:T(8,128)(2,1)S(1)}, u32[]{:S(2)}, u32[]{:S(2)}) collective-permute-start(bf16[32,128,128]{2,1,0:T(8,128)(2,1)} %bitcast.9), channel_id=1, source_target_pairs={{32,0},{33,1},{34,2},{35,3},{36,4},{37,5},{38,6},{39,7},{40,8},{41... | collective-permute-start | bytes 3145736 | tf_op jit(solution)/shard_map/ppermute | solution.py:182
  29.1 82.2 %collective-permute-start.34 = (bf16[24,128,128]{2,1,0:T(8,128)(2,1)}, bf16[24,128,128]{2,1,0:T(8,128)(2,1)S(1)}, u32[]{:S(2)}, u32[]{:S(2)}) collective-permute-start(bf16[24,128,128]{2,1,0:T(8,128)(2,1)} %bitcast.43), channel_id=1, source_target_pairs={{1,0},{2,1},{3,2},{4,3},{5,4},{6,5},{7,6},{8,7},{9,8},{10,9},{11,1... | collective-permute-start | bytes 2359304 | tf_op jit(solution)/shard_map/ppermute | solution.py:180
  37.2 15.7 %collective-permute-start.35 = (s32[48]{0:T(128)S(1)}, s32[48]{0:T(128)S(1)}, u32[]{:S(2)}, u32[]{:S(2)}) collective-permute-start(s32[48]{0:T(128)S(1)} %pad_add_fusion), channel_id=1, source_target_pairs={{32,64},{33,65},{34,66},{35,67},{36,68},{37,69},{38,70},{39,71},{4... | collective-permute-start | bytes 584 | tf_op jit(solution)/shard_map/ppermute | solution.py:178
  55.9 1.6 %copy-start.4 = (bf16[32,128,128]{2,1,0:T(8,128)(2,1)S(1)}, bf16[32,128,128]{2,1,0:T(8,128)(2,1)}, u32[]{:S(2)}) copy-start(bf16[32,128,128]{2,1,0:T(8,128)(2,1)} %get-tuple-element.859.right_blocks) | copy-start | bytes 3145732 | tf_op jit(solution)/shard_map/cond
  56.0 53.7 %collective-permute-start.21 = (bf16[22,128,128]{2,1,0:T(8,128)(2,1)S(1)}, bf16[22,128,128]{2,1,0:T(8,128)(2,1)S(1)}, u32[]{:S(2)}, u32[]{:S(2)}) collective-permute-start(bf16[22,128,128]{2,1,0:T(8,128)(2,1)S(1)} %slice.85), channel_id=1, source_target_pairs={{64,32},{65,33},{66,34},{67,35},{68,36},{69,37},{70,38},{71,39},{7... | collective-permute-start | bytes 2162696 | tf_op jit(solution)/shard_map/cond/branch_21_fun/ppermute | solution.py:203
